TPU v7x, 32 devices: a whole 2x2x4 slice. The times are simulated.
32 devices in a mesh: dom: 8 (over y, x, core), tm: 4 (over z).
Axes of the slice: x: 2, y: 2, z: 4, core: 2. Of those that a mesh axis runs over, the one named last changes fastest.
Arguments:
- features: bfloat16 [4, 2048, 512], P('tm', 'dom'), may hold values from -6 to 6
- tile_rows: int32 [4, 192], P('tm', 'dom'), may hold values from 0 to 15, as said below
- tile_cols: int32 [4, 192], P('tm', 'dom'), may hold values from 0 to 15, as said below
- tile_vals: bfloat16 [4, 192, 128, 128], P('tm', 'dom'), may hold values from 0 to 0.0625
- tile_used: int32 [4, 8], P('tm', 'dom'), may hold values from 12 to 24, as said below
- pool_weight: bfloat16 [512, 512], replicated, may hold values from -0.25 to 0.25
- w_in: bfloat16 [3, 512, 512], replicated, may hold values from -0.25 to 0.25
- w_state: bfloat16 [3, 512, 512], replicated, may hold values from -0.25 to 0.25
- gate_offset: float32 [512], replicated, may hold values from 0 to 5
- start_weight: float32 [512, 512], replicated, may hold values from -3 to 3
Outputs:
- hidden_out: bfloat16 [4, 2048, 512], P('tm', 'dom')
- weights_out: float32 [4, 512, 512], P('tm')
Inputs may be any that keep to these rules, and one draw needn't show every extreme that they name: `tile_rows`: every slot of row partition d names a row block of that partition, d * 2 to (d + 1) * 2 - 1. `tile_cols`: within one snapshot and one row partition, all slots whose column blocks lie on the same dom index name the same column block. `tile_used`: in every snapshot some row partition has all 24 slots live.
All inputs are finite; a program needn't handle non-finite values.
Results may differ from a plain program's by a relative error of at most 0.017.
Values may be sent and summed in bfloat16 or wider, within the bound.
A program may use at most 64 MiB of HBM per device.

v0:
```python
import functools

import jax
import jax.numpy as jnp
from jax import lax
from jax.experimental import pallas as pl
from jax.experimental.pallas import tpu as pltpu
from jax.sharding import PartitionSpec as P

BLOCK = 128
LANES = 128
CORES = 2


def xor(q, k, bits):
    out = 0
    for b in range(bits):
        out = out + (((q // (1 << b)) + ((k >> b) & 1)) % 2) * (1 << b)
    return out


def nt_dot(a, b):
    return lax.dot_general(a, b, (((1,), (1,)), ((), ())), preferred_element_type=jnp.float32)


def tn_dot(a, b):
    return lax.dot_general(a, b, (((0,), (0,)), ((), ())), preferred_element_type=jnp.float32)


def kernel(
    n_dom,
    n_tm,
    feats_ref,
    rows_ref,
    cols_ref,
    vals_ref,
    used_ref,
    pool_ref,
    win_ref,
    wst_ref,
    off_ref,
    start_ref,
    hid_ref,
    wout_ref,
    feats,
    vals,
    pool,
    win,
    wst,
    off,
    state,
    sums,
    wfull,
    agg,
    load_sem,
    f_send,
    f_recv,
    ff_send,
    ff_recv,
    z_send,
    z_recv,
    zf_send,
    zf_recv,
    w_send,
    w_recv,
    wf_send,
    wf_recv,
):
    n_chips = n_dom // CORES
    bits = n_chips.bit_length() - 1
    blocks, _, width = feats_ref.shape
    slots = vals_ref.shape[0]
    groups = wfull.shape[0]
    half_k = LANES // CORES
    half_r = width // CORES
    rows_dev = blocks * BLOCK
    me = lax.axis_index("dom")
    t_me = lax.axis_index("tm")
    chip, core = me // CORES, me % CORES
    group = chip % groups
    partner = {"dom": chip * CORES + 1 - core}
    lane0 = pl.multiple_of(group * LANES, LANES)

    def same_core(k):
        return {"dom": xor(chip, k, bits) * CORES + core}

    def remote(src, dst, send, recv, to):
        return pltpu.make_async_remote_copy(
            src_ref=src, dst_ref=dst, send_sem=send, recv_sem=recv,
            device_id=to, device_id_type=pl.DeviceIdType.MESH,
        )

    def load(src, dst, i):
        copy = pltpu.make_async_copy(src, dst, load_sem.at[i])
        copy.start()
        return copy

    def piece(dev):
        return feats.at[pl.ds(dev * blocks, blocks)]

    loads = [
        load(feats_ref, piece(me), 0),
        load(pool_ref.at[:, pl.ds(lane0, LANES)], pool, 1),
        load(vals_ref, vals, 2),
        load(win_ref, win, 3),
        load(wst_ref, wst, 4),
        load(start_ref.at[:, pl.ds(lane0, LANES)], state, 5),
        load(off_ref, off, 6),
    ]

    barrier = pltpu.get_barrier_semaphore()
    greet = [partner] + [same_core(k) for k in range(1, n_chips)]
    greet += [{"tm": (t_me + o) % n_tm} for o in range(1, n_tm)]
    for to in greet:
        pl.semaphore_signal(barrier, inc=1, device_id=to, device_id_type=pl.DeviceIdType.MESH)
    pl.semaphore_wait(barrier, len(greet))

    f_out = [None] + [
        remote(feats_ref, piece(me), f_send.at[k], f_recv.at[k], same_core(k))
        for k in range(1, n_chips)
    ]
    for k in range(1, n_chips):
        f_out[k].start()
    ff_out = [remote(feats_ref, piece(me), ff_send.at[0], ff_recv.at[0], partner)]
    ff_out[0].start()

    loads[0].wait()
    loads[1].wait()

    def pooled(dev):
        f = feats[pl.ds(dev * blocks, blocks)].reshape(rows_dev, width)
        gates = jax.nn.sigmoid(jnp.dot(f, pool[...], preferred_element_type=jnp.float32))
        return tn_dot(gates.astype(jnp.bfloat16), f)

    total = pooled(me)
    ff_out[0].wait_recv()
    total = total + pooled(chip * CORES + 1 - core)
    for k in range(1, n_chips):
        dev = xor(chip, k, bits) * CORES
        f_out[k].wait_recv()
        ff_out.append(
            remote(piece(dev + core), piece(dev + core), ff_send.at[k], ff_recv.at[k], partner)
        )
        ff_out[k].start()
        total = total + pooled(dev + core)
    for k in range(1, n_chips):
        dev = xor(chip, k, bits) * CORES
        ff_out[k].wait_recv()
        total = total + pooled(dev + 1 - core)
    sums[t_me] = (total * (rows_dev * n_dom) ** (-0.5)).astype(jnp.bfloat16)

    my_half = pl.ds(core * half_k, half_k)
    z_out = []
    for o in range(1, n_tm):
        z_out.append(
            remote(
                sums.at[t_me, my_half], sums.at[t_me, my_half],
                z_send.at[o], z_recv.at[t_me], {"tm": (t_me + o) % n_tm},
            )
        )
        z_out[-1].start()

    loads[2].wait()
    masked = []
    sources = []
    for j in range(slots):
        tile = vals[j]
        live = j < used_ref[0, 0]
        row = rows_ref[0, j] - me * blocks
        masked.append(
            jnp.concatenate(
                [jnp.where(live & (row == b), tile, jnp.zeros_like(tile)) for b in range(blocks)],
                axis=0,
            )
        )
        sources.append(feats[cols_ref[0, j]])
    own = feats[pl.ds(me * blocks, blocks)].reshape(rows_dev, width).astype(jnp.float32)
    summed = jnp.dot(
        jnp.concatenate(masked, axis=1),
        jnp.concatenate(sources, axis=0),
        preferred_element_type=jnp.float32,
    )
    agg[...] = (own + summed).astype(jnp.bfloat16)

    def z_forward(t):
        ref = sums.at[t, my_half]
        return remote(ref, ref, zf_send.at[t], zf_recv.at[t], partner)

    for t in range(n_tm):
        @pl.when(t_me != t)
        def _(t=t):
            ref = sums.at[t, my_half]
            remote(ref, ref, z_send.at[0], z_recv.at[t], partner).wait_recv()
            z_forward(t).start()

    for i in range(3, 7):
        loads[i].wait()
    offset = jnp.transpose(jnp.broadcast_to(off[...], (LANES, width)))
    for t in range(n_tm):
        @pl.when(t_me != t)
        def _(t=t):
            z_forward(t).wait_recv()

        summary = sums[t]
        now = state[...]
        now_b = now.astype(jnp.bfloat16)
        reset = jax.nn.sigmoid(
            nt_dot(win[1], summary) + jnp.dot(wst[1], now_b, preferred_element_type=jnp.float32)
        )
        reset_state = (reset * now).astype(jnp.bfloat16)
        update = jax.nn.sigmoid(
            nt_dot(win[0], summary)
            + jnp.dot(wst[0], now_b, preferred_element_type=jnp.float32)
            - offset
        )
        candidate = jnp.tanh(
            nt_dot(win[2], summary)
            + jnp.dot(wst[2], reset_state, preferred_element_type=jnp.float32)
        )
        new = (1.0 - update) * now + update * candidate
        state[...] = new

        @pl.when(t_me == t)
        def _(new=new):
            wfull[group] = new.astype(jnp.bfloat16)

    w_half = pl.ds(core * half_r, half_r)
    w_out = [None]
    for k in range(1, groups):
        ref = wfull.at[group, w_half]
        w_out.append(remote(ref, ref, w_send.at[k], w_recv.at[k], same_core(k)))
        w_out[k].start()

    def emit(g):
        w = wfull[g]
        lanes = pl.ds(pl.multiple_of(g * LANES, LANES), LANES)
        mixed = jnp.dot(agg[...], w, preferred_element_type=jnp.float32)
        hid_ref[:, lanes] = jnp.maximum(mixed * width ** (-0.5), 0.0).astype(jnp.bfloat16)
        wout_ref[:, lanes] = w.astype(jnp.float32)

    emit(group)
    wf_out = [None]
    for k in range(1, groups):
        w_out[k].wait_recv()
        ref = wfull.at[xor(group, k, bits), w_half]
        wf_out.append(remote(ref, ref, wf_send.at[k], wf_recv.at[k], partner))
        wf_out[k].start()
    for k in range(1, groups):
        wf_out[k].wait_recv()
        emit(xor(group, k, bits))

    for k in range(1, n_chips):
        f_out[k].wait_send()
    for k in range(n_chips):
        ff_out[k].wait_send()
    for copy in z_out:
        copy.wait_send()
    for t in range(n_tm):
        @pl.when(t_me != t)
        def _(t=t):
            z_forward(t).wait_send()
    for k in range(1, groups):
        w_out[k].wait_send()
        wf_out[k].wait_send()


def shards(
    n_dom,
    n_tm,
    features,
    tile_rows,
    tile_cols,
    tile_vals,
    tile_used,
    pool_weight,
    w_in,
    w_state,
    gate_offset,
    start_weight,
):
    _, rows_dev, width = features.shape
    slots = tile_rows.shape[1]
    blocks = rows_dev // BLOCK
    n_chips = n_dom // CORES
    groups = width // LANES
    hbm = pl.BlockSpec(memory_space=pl.ANY)
    smem = pl.BlockSpec(memory_space=pltpu.SMEM)
    vmem = pl.BlockSpec(memory_space=pltpu.VMEM)
    dma = pltpu.SemaphoreType.DMA
    bf16 = jnp.bfloat16
    hidden, weights = pl.pallas_call(
        functools.partial(kernel, n_dom, n_tm),
        out_shape=(
            jax.ShapeDtypeStruct((rows_dev, width), bf16),
            jax.ShapeDtypeStruct((width, width), jnp.float32),
        ),
        in_specs=[hbm, smem, smem, hbm, smem, hbm, hbm, hbm, hbm, hbm],
        out_specs=(vmem, vmem),
        scratch_shapes=[
            pltpu.VMEM((n_dom * blocks, BLOCK, width), bf16),
            pltpu.VMEM((slots, BLOCK, BLOCK), bf16),
            pltpu.VMEM((width, LANES), bf16),
            pltpu.VMEM((3, width, width), bf16),
            pltpu.VMEM((3, width, width), bf16),
            pltpu.VMEM((1, width), jnp.float32),
            pltpu.VMEM((width, LANES), jnp.float32),
            pltpu.VMEM((n_tm, LANES, width), bf16),
            pltpu.VMEM((groups, width, LANES), bf16),
            pltpu.VMEM((rows_dev, width), bf16),
            dma((7,)),
            dma((n_chips,)),
            dma((n_chips,)),
            dma((n_chips,)),
            dma((n_chips,)),
            dma((n_tm,)),
            dma((n_tm,)),
            dma((n_tm,)),
            dma((n_tm,)),
            dma((groups,)),
            dma((groups,)),
            dma((groups,)),
            dma((groups,)),
        ],
        compiler_params=pltpu.CompilerParams(
            collective_id=0, has_side_effects=True, vmem_limit_bytes=48 * 1024 * 1024
        ),
    )(
        features.reshape(blocks, BLOCK, width),
        tile_rows,
        tile_cols,
        tile_vals.reshape(slots, BLOCK, BLOCK),
        tile_used,
        pool_weight,
        w_in,
        w_state,
        gate_offset.reshape(1, width),
        start_weight,
    )
    return hidden[None], weights[None]


def solution(mesh):
    in_specs = (
        P("tm", "dom", None),
        P("tm", "dom"),
        P("tm", "dom"),
        P("tm", "dom", None, None),
        P("tm", "dom"),
        P(),
        P(),
        P(),
        P(),
        P(),
    )
    out_specs = (P("tm", "dom", None), P("tm", None, None))
    body = functools.partial(shards, mesh.shape["dom"], mesh.shape["tm"])
    return jax.shard_map(body, mesh=mesh, in_specs=in_specs, out_specs=out_specs, check_vma=False)
```

profile of v0, /device:TPU:0, one launch (start us, length us, event | category | flops | bytes accessed | tf_op | source)
XLA Modules:
  0.0 50.1 jit_solution(14083133225401438677)
XLA Ops:
  1.3 0.0 copy-start
  1.3 1.4 %copy-done = bf16[3,512,512]{2,1,0:T(8,128)(2,1)S(1)} copy-done((bf16[3,512,512]{2,1,0:T(8,128)(2,1)S(1)}, bf16[3,512,512]{2,1,0:T(8,128)(2,1)}, u32[]{:S(2)}) %copy-start) | copy-done | bytes 1572888
  2.7 0.0 copy-start.1
  2.7 1.2 %copy-done.1 = f32[512,512]{1,0:T(8,128)S(1)} copy-done((f32[512,512]{1,0:T(8,128)S(1)}, f32[512,512]{1,0:T(8,128)}, u32[]{:S(2)}) %copy-start.1) | copy-done | bytes 1048600
  3.9 0.0 copy-start.2
  3.9 1.1 %copy-done.2 = bf16[1,24,128,128]{3,2,1,0:T(8,128)(2,1)S(1)} copy-done((bf16[1,24,128,128]{3,2,1,0:T(8,128)(2,1)S(1)}, bf16[1,24,128,128]{3,2,1,0:T(8,128)(2,1)}, u32[]{:S(2)}) %copy-start.2) | copy-done | bytes 786456
  5.0 0.0 copy-start.3
  5.0 1.0 %copy-done.3 = bf16[512,512]{1,0:T(8,128)(2,1)S(1)} copy-done((bf16[512,512]{1,0:T(8,128)(2,1)S(1)}, bf16[512,512]{1,0:T(8,128)(2,1)}, u32[]{:S(2)}) %copy-start.3) | copy-done | bytes 524312
  6.1 0.0 copy-start.4
  6.1 0.9 %copy-done.4 = bf16[1,256,512]{2,1,0:T(8,128)(2,1)S(1)} copy-done((bf16[1,256,512]{2,1,0:T(8,128)(2,1)S(1)}, bf16[1,256,512]{2,1,0:T(8,128)(2,1)}, u32[]{:S(2)}) %copy-start.4) | copy-done | bytes 262168
  7.0 0.0 copy-start.5
  7.0 0.7 %copy-done.5 = f32[512]{0:T(512)S(1)} copy-done((f32[512]{0:T(512)S(1)}, f32[512]{0:T(512)}, u32[]{:S(2)}) %copy-start.5) | copy-done | bytes 2072
  7.7 0.0 copy-start.6
  7.7 0.7 %copy-done.6 = s32[1,24]{1,0:T(1,128)S(1)} copy-done((s32[1,24]{1,0:T(1,128)S(1)}, s32[1,24]{1,0:T(1,128)}, u32[]{:S(2)}) %copy-start.6) | copy-done | bytes 120
  8.4 0.0 copy-start.7
  8.4 0.7 %copy-done.7 = s32[1,24]{1,0:T(1,128)S(1)} copy-done((s32[1,24]{1,0:T(1,128)S(1)}, s32[1,24]{1,0:T(1,128)}, u32[]{:S(2)}) %copy-start.7) | copy-done | bytes 120
  9.0 39.4 %shard_map.113 = (bf16[256,512]{1,0:T(8,128)(2,1)S(1)}, f32[512,512]{1,0:T(8,128)S(1)}) custom-call(bf16[2,128,512]{2,1,0:T(8,128)(2,1)S(1)} %bitcast.7, s32[1,24]{1,0:T(1,128)S(1)} %copy-done.6, s32[1,24]{1,0:T(1,128)S(1)} %copy-done.7, bf16[24,128,128]{2,1,0:T(8,128)(2,1)S(1)} %bitcast.6, s32[1,1]{1,0:T(1,128)S(6)} %copy.14.used_ref, ...), custom_call_target="tpu_custom_call" | custom-call | tf_op jit(solution)/shard_map/pallas_call | solution.py:291
  48.4 0.7 %copy.15 = bf16[1,256,512]{2,1,0:T(8,128)(2,1)} copy(bf16[1,256,512]{2,1,0:T(8,128)(2,1)S(1)} %bitcast.8) | data formatting | bytes 524288
  49.1 1.0 %copy.16 = f32[1,512,512]{2,1,0:T(8,128)} copy(f32[1,512,512]{2,1,0:T(8,128)S(1)} %bitcast.5) | data formatting | bytes 2097152
Async XLA Ops:
  1.3 1.4 %copy-start = (bf16[3,512,512]{2,1,0:T(8,128)(2,1)S(1)}, bf16[3,512,512]{2,1,0:T(8,128)(2,1)}, u32[]{:S(2)}) copy-start(bf16[3,512,512]{2,1,0:T(8,128)(2,1)} %win_ref.1) | copy-start | bytes 4718596
  2.7 1.2 %copy-start.1 = (f32[512,512]{1,0:T(8,128)S(1)}, f32[512,512]{1,0:T(8,128)}, u32[]{:S(2)}) copy-start(f32[512,512]{1,0:T(8,128)} %start_ref.1) | copy-start | bytes 3145732
  3.9 1.1 %copy-start.2 = (bf16[1,24,128,128]{3,2,1,0:T(8,128)(2,1)S(1)}, bf16[1,24,128,128]{3,2,1,0:T(8,128)(2,1)}, u32[]{:S(2)}) copy-start(bf16[1,24,128,128]{3,2,1,0:T(8,128)(2,1)} %param.13) | copy-start | bytes 2359300
  5.0 1.0 %copy-start.3 = (bf16[512,512]{1,0:T(8,128)(2,1)S(1)}, bf16[512,512]{1,0:T(8,128)(2,1)}, u32[]{:S(2)}) copy-start(bf16[512,512]{1,0:T(8,128)(2,1)} %pool_ref.1) | copy-start | bytes 1572868
  6.1 0.9 %copy-start.4 = (bf16[1,256,512]{2,1,0:T(8,128)(2,1)S(1)}, bf16[1,256,512]{2,1,0:T(8,128)(2,1)}, u32[]{:S(2)}) copy-start(bf16[1,256,512]{2,1,0:T(8,128)(2,1)} %param.10) | copy-start | bytes 786436
  7.0 0.7 %copy-start.5 = (f32[512]{0:T(512)S(1)}, f32[512]{0:T(512)}, u32[]{:S(2)}) copy-start(f32[512]{0:T(512)} %param.18) | copy-start | bytes 6148
  7.7 0.7 %copy-start.6 = (s32[1,24]{1,0:T(1,128)S(1)}, s32[1,24]{1,0:T(1,128)}, u32[]{:S(2)}) copy-start(s32[1,24]{1,0:T(1,128)} %rows_ref.1) | copy-start | bytes 292
  8.4 0.7 %copy-start.7 = (s32[1,24]{1,0:T(1,128)S(1)}, s32[1,24]{1,0:T(1,128)}, u32[]{:S(2)}) copy-start(s32[1,24]{1,0:T(1,128)} %cols_ref.1) | copy-start | bytes 292
where the time goes:
time: 50.6 us; the launch traced here: 50.1 us
  Pallas kernels  39.4 us (78%)
  local copies, waits for them, and re-layouts  9.41 us (19%)
  between operations  1.3 us (3%)
    pallas_call x1, Pallas kernels, shards(): pl.pallas_call(functools.partial(kernel, n_dom, n_tm), out_shape=(jax.Sha...  39.4 us
    unnamed x18, local copies, waits for them, and re-layouts  9.41 us

commit v1 on v0

v1 whole, which is shorter than its diff:
```python
import functools

import jax
import jax.numpy as jnp
from jax import lax
from jax.experimental import pallas as pl
from jax.experimental.pallas import tpu as pltpu
from jax.sharding import PartitionSpec as P

BLOCK = 128
LANES = 128
CORES = 2


def xor(q, k, bits):
    out = 0
    for b in range(bits):
        out = out + (((q // (1 << b)) + ((k >> b) & 1)) % 2) * (1 << b)
    return out


def nt_dot(a, b):
    return lax.dot_general(a, b, (((1,), (1,)), ((), ())), preferred_element_type=jnp.float32)


def tn_dot(a, b):
    return lax.dot_general(a, b, (((0,), (0,)), ((), ())), preferred_element_type=jnp.float32)


def kernel(
    n_dom,
    n_tm,
    feats_ref,
    rows_in,
    cols_in,
    vals_ref,
    used_in,
    pool_ref,
    win_ref,
    wst_ref,
    off_ref,
    start_ref,
    hid_ref,
    wout_ref,
    feats,
    vals,
    pool,
    win,
    wst,
    off,
    start,
    part,
    part_b,
    pair_in,
    reduced,
    terms,
    sums,
    wfull,
    agg,
    mask,
    rows_ref,
    cols_ref,
    used_ref,
    load_sem,
    pair_sem,
    r_send,
    r_recv,
    f_send,
    f_recv,
    ff_send,
    ff_recv,
    z_send,
    z_recv,
    w_send,
    w_recv,
    wf_send,
    wf_recv,
):
    n_chips = n_dom // CORES
    bits = n_chips.bit_length() - 1
    blocks, _, width = feats_ref.shape
    slots = vals_ref.shape[0]
    groups = wfull.shape[0]
    half = LANES // CORES
    rows_dev = blocks * BLOCK
    me = lax.axis_index("dom")
    t_me = lax.axis_index("tm")
    chip, core = me // CORES, me % CORES
    group = chip % groups
    partner = {"dom": chip * CORES + 1 - core}
    lane0 = pl.multiple_of(group * LANES, LANES)

    def same_core(k):
        return {"dom": xor(chip, k, bits) * CORES + core}

    def remote(src, dst, send, recv, to):
        return pltpu.make_async_remote_copy(
            src_ref=src, dst_ref=dst, send_sem=send, recv_sem=recv,
            device_id=to, device_id_type=pl.DeviceIdType.MESH,
        )

    def load(src, dst, i):
        copy = pltpu.make_async_copy(src, dst, load_sem.at[i])
        copy.start()
        return copy

    def piece(dev):
        return feats.at[pl.ds(dev * blocks, blocks)]

    loads = [
        load(feats_ref, piece(me), 0),
        load(pool_ref, pool, 1),
        load(start_ref.at[:, pl.ds(lane0, LANES)], start, 2),
        load(win_ref, win, 3),
        load(wst_ref, wst, 4),
        load(off_ref, off, 5),
        load(vals_ref, vals, 6),
        load(rows_in, rows_ref, 7),
        load(cols_in, cols_ref, 8),
        load(used_in, used_ref, 9),
    ]

    barrier = pltpu.get_barrier_semaphore()
    greet = [partner] + [same_core(k) for k in range(1, n_chips)]
    greet += [{"tm": (t_me + o) % n_tm} for o in range(1, n_tm)]
    for to in greet:
        pl.semaphore_signal(barrier, inc=1, device_id=to, device_id_type=pl.DeviceIdType.MESH)

    orders = [list(range(bits)) if b % 2 == 0 else list(range(bits))[::-1] for b in range(blocks)]
    f_out, ff_out = {}, {}

    def forward(b, m):
        src = feats_ref.at[b] if m == 0 else slot(b, m)
        ff_out[b, m] = remote(src, slot(b, m), ff_send.at[b, m], ff_recv.at[b, m], partner)
        ff_out[b, m].start()

    def slot(b, m):
        return feats.at[(xor(chip, m, bits) * CORES + core) * blocks + b]

    def arrive(b, m):
        f_out[b, m].wait_recv()
        forward(b, m)

    def gather_stage(i):
        for b in range(blocks):
            held = [0]
            for d in orders[b][:i]:
                held = held + [m + (1 << d) for m in held]
            step = 1 << orders[b][i]
            for m in held:
                if m and (b, m) not in ff_out:
                    arrive(b, m)
                src = feats_ref.at[b] if m == 0 else slot(b, m)
                n = m + step
                f_out[b, n] = remote(src, slot(b, m), f_send.at[b, n], f_recv.at[b, n], same_core(step))
                f_out[b, n].start()

    loads[0].wait()
    loads[1].wait()
    f = feats[pl.ds(me * blocks, blocks)].reshape(rows_dev, width)
    gates = jax.nn.sigmoid(jnp.dot(f, pool[...], preferred_element_type=jnp.float32))
    pl.semaphore_wait(barrier, len(greet))
    gather_stage(0)
    pooled = tn_dot(gates.astype(jnp.bfloat16), f).reshape(groups, CORES, half, width)
    for h in range(CORES):
        part[h] = pooled[:, h]
        part_b[h] = pooled[:, h].astype(jnp.bfloat16)

    pair = remote(part_b.at[1 - core], pair_in, pair_sem.at[0], pair_sem.at[1], partner)
    pair.start()
    pair.wait_recv()
    part[core] = part[core] + pair_in[...].astype(jnp.float32)
    reduced[...] = part[core].astype(jnp.bfloat16)
    r_out = [None]
    for k in range(1, n_chips):
        to = xor(chip, k, bits)
        r_out.append(
            remote(reduced.at[to % groups], terms.at[k], r_send.at[k], r_recv.at[k], same_core(k))
        )
        r_out[k].start()
    for b in range(blocks):
        forward(b, 0)

    loads[2].wait()
    turned = jnp.transpose(start[...])
    state = jnp.where(core == 0, turned[:half], turned[half:])
    total = part[core, group]
    for k in range(1, n_chips):
        r_out[k].wait_recv()
        total = total + terms[k].astype(jnp.float32)
    sums[t_me] = (total * (rows_dev * n_dom) ** (-0.5)).astype(jnp.bfloat16)

    z_out = []
    for o in range(1, n_tm):
        z_out.append(
            remote(
                sums.at[t_me], sums.at[t_me], z_send.at[o], z_recv.at[t_me],
                {"tm": (t_me + o) % n_tm},
            )
        )
        z_out[-1].start()

    for i in range(1, bits):
        gather_stage(i)

    for i in range(3, 10):
        loads[i].wait()
    for j in range(slots):
        tile = vals[j]
        live = j < used_ref[0, 0]
        row = rows_ref[0, j] - me * blocks
        for b in range(blocks):
            mask[b * BLOCK:(b + 1) * BLOCK, j * BLOCK:(j + 1) * BLOCK] = jnp.where(
                live & (row == b), tile, jnp.zeros_like(tile)
            )
    for t in range(n_tm):
        @pl.when(t_me != t)
        def _(t=t):
            remote(sums.at[t], sums.at[t], z_send.at[0], z_recv.at[t], partner).wait_recv()

    every = sums[...].reshape(n_tm * half, width)
    inputs = [nt_dot(every, win[g]).reshape(n_tm, half, width) for g in range(3)]
    own_w = wfull.at[group, pl.ds(core * half, half)]
    for t in range(n_tm):
        state_b = state.astype(jnp.bfloat16)
        reset = jax.nn.sigmoid(inputs[1][t] + nt_dot(state_b, wst[1]))
        reset_state = (reset * state).astype(jnp.bfloat16)
        update = jax.nn.sigmoid(inputs[0][t] + nt_dot(state_b, wst[0]) - off[...])
        candidate = jnp.tanh(inputs[2][t] + nt_dot(reset_state, wst[2]))
        state = (1.0 - update) * state + update * candidate

        @pl.when(t_me == t)
        def _(state=state):
            own_w[...] = state.astype(jnp.bfloat16)

    w_out = [None]
    for k in range(1, groups):
        w_out.append(remote(own_w, own_w, w_send.at[k], w_recv.at[k], same_core(k)))
        w_out[k].start()
    wf_out = [remote(own_w, own_w, wf_send.at[0], wf_recv.at[0], partner)]
    wf_out[0].start()

    for key in list(f_out):
        if key not in ff_out:
            arrive(*key)
    for copy in ff_out.values():
        copy.wait_recv()
    sources = [feats[cols_ref[0, j]] for j in range(slots)]
    own = feats[pl.ds(me * blocks, blocks)].reshape(rows_dev, width).astype(jnp.float32)
    summed = jnp.dot(
        mask[...],
        jnp.concatenate(sources, axis=0),
        preferred_element_type=jnp.float32,
    )
    agg[...] = (own + summed).astype(jnp.bfloat16)

    for k in range(1, groups):
        w_out[k].wait_recv()
        ref = wfull.at[xor(group, k, bits), pl.ds(core * half, half)]
        wf_out.append(remote(ref, ref, wf_send.at[k], wf_recv.at[k], partner))
        wf_out[k].start()
    for k in range(groups):
        wf_out[k].wait_recv()
        g = xor(group, k, bits)
        w = wfull[g]
        lanes = pl.ds(pl.multiple_of(g * LANES, LANES), LANES)
        mixed = nt_dot(agg[...], w)
        hid_ref[:, lanes] = jnp.maximum(mixed * width ** (-0.5), 0.0).astype(jnp.bfloat16)
        wout_ref[:, lanes] = jnp.transpose(w.astype(jnp.float32))

    pair.wait_send()
    for copy in (
        r_out[1:] + list(f_out.values()) + list(ff_out.values()) + z_out + w_out[1:] + wf_out
    ):
        copy.wait_send()


def shards(
    n_dom,
    n_tm,
    features,
    tile_rows,
    tile_cols,
    tile_vals,
    tile_used,
    pool_weight,
    w_in,
    w_state,
    gate_offset,
    start_weight,
):
    _, rows_dev, width = features.shape
    slots = tile_rows.shape[1]
    blocks = rows_dev // BLOCK
    n_chips = n_dom // CORES
    groups = width // LANES
    hbm = pl.BlockSpec(memory_space=pltpu.HBM)
    vmem = pl.BlockSpec(memory_space=pltpu.VMEM)
    dma = pltpu.SemaphoreType.DMA
    bf16, f32 = jnp.bfloat16, jnp.float32
    half = LANES // CORES
    hidden, weights = pl.pallas_call(
        functools.partial(kernel, n_dom, n_tm),
        out_shape=(
            jax.ShapeDtypeStruct((rows_dev, width), bf16),
            jax.ShapeDtypeStruct((width, width), jnp.float32),
        ),
        in_specs=[hbm] * 10,
        out_specs=(vmem, vmem),
        scratch_shapes=[
            pltpu.VMEM((n_dom * blocks, BLOCK, width), bf16),
            pltpu.VMEM((slots, BLOCK, BLOCK), bf16),
            pltpu.VMEM((width, width), bf16),
            pltpu.VMEM((3, width, width), bf16),
            pltpu.VMEM((3, width, width), bf16),
            pltpu.VMEM((1, width), f32),
            pltpu.VMEM((width, LANES), f32),
            pltpu.VMEM((CORES, groups, half, width), f32),
            pltpu.VMEM((CORES, groups, half, width), bf16),
            pltpu.VMEM((groups, half, width), bf16),
            pltpu.VMEM((groups, half, width), bf16),
            pltpu.VMEM((n_chips, half, width), bf16),
            pltpu.VMEM((n_tm, half, width), bf16),
            pltpu.VMEM((groups, LANES, width), bf16),
            pltpu.VMEM((rows_dev, width), bf16),
            pltpu.VMEM((rows_dev, slots * BLOCK), bf16),
            pltpu.SMEM((1, slots), jnp.int32),
            pltpu.SMEM((1, slots), jnp.int32),
            pltpu.SMEM((1, 1), jnp.int32),
            dma((10,)),
            dma((2,)),
            dma((n_chips,)),
            dma((n_chips,)),
            dma((blocks, n_chips)),
            dma((blocks, n_chips)),
            dma((blocks, n_chips)),
            dma((blocks, n_chips)),
            dma((n_tm,)),
            dma((n_tm,)),
            dma((groups,)),
            dma((groups,)),
            dma((groups,)),
            dma((groups,)),
        ],
        compiler_params=pltpu.CompilerParams(
            collective_id=0, has_side_effects=True, vmem_limit_bytes=60 * 1024 * 1024
        ),
    )(
        features.reshape(blocks, BLOCK, width),
        tile_rows,
        tile_cols,
        tile_vals.reshape(slots, BLOCK, BLOCK),
        tile_used,
        pool_weight,
        w_in,
        w_state,
        gate_offset.reshape(1, width),
        start_weight,
    )
    return hidden[None], weights[None]


def solution(mesh):
    in_specs = (
        P("tm", "dom", None),
        P("tm", "dom"),
        P("tm", "dom"),
        P("tm", "dom", None, None),
        P("tm", "dom"),
        P(),
        P(),
        P(),
        P(),
        P(),
    )
    out_specs = (P("tm", "dom", None), P("tm", None, None))
    body = functools.partial(shards, mesh.shape["dom"], mesh.shape["tm"])
    return jax.shard_map(body, mesh=mesh, in_specs=in_specs, out_specs=out_specs, check_vma=False)
```

time: 50.6 us -> 35.2 us (0.70)
  Pallas kernels: 39.4 us -> 29.8 us
  local copies, waits for them, and re-layouts: 9.41 us -> 3.93 us
    pallas_call x1, Pallas kernels: 39.4 us -> 29.8 us  [shards(): pl.pallas_call(functools.partial(kernel, n_dom, n_tm), out_shape=(jax.Sha...]
    unnamed x18 -> x2, local copies, waits for them, and re-layouts: 9.41 us -> 3.93 us
where the time goes in v1:
time: 35.2 us; the launch traced here: 35 us
  Pallas kernels  29.8 us (85%)
  local copies, waits for them, and re-layouts  3.93 us (11%)
  between operations  1.29 us (4%)
    pallas_call x1, Pallas kernels, shards(): pl.pallas_call(functools.partial(kernel, n_dom, n_tm), out_shape=(jax.Sha...  29.8 us
    unnamed x2, local copies, waits for them, and re-layouts  3.93 us

profile of v1, /device:TPU:0, one launch (start us, length us, event | category | flops | bytes accessed | tf_op | source)
XLA Modules:
  0.0 35.0 jit_solution(11481732116052883143)
XLA Ops:
  1.3 29.8 %shard_map.113 = (bf16[256,512]{1,0:T(8,128)(2,1)}, f32[512,512]{1,0:T(8,128)}) custom-call(bf16[2,128,512]{2,1,0:T(8,128)(2,1)} %bitcast.7, s32[1,24]{1,0:T(1,128)} %rows_in.1, s32[1,24]{1,0:T(1,128)} %cols_in.1, bf16[24,128,128]{2,1,0:T(8,128)(2,1)} %bitcast.6, s32[1,1]{1,0:T(1,128)S(6)} %copy.14.used_in, bf16[512,512]{1,0:T(8,128)(2,1)} %pool_ref.1, ...), custom_call_target="tpu_custom_call" | custom-call | tf_op jit(solution)/shard_map/pallas_call | solution.py:302
  31.1 1.7 %copy.15 = bf16[1,256,512]{2,1,0:T(8,128)(2,1)} copy(bf16[1,256,512]{2,1,0:T(8,128)(2,1)} %bitcast.8) | data formatting | bytes 524288
  32.7 2.3 %copy.16 = f32[1,512,512]{2,1,0:T(8,128)} copy(f32[1,512,512]{2,1,0:T(8,128)} %bitcast.5) | data formatting | bytes 2097152

commit v2 on v1

--- a/solution.py
+++ b/solution.py
@@ -275,6 +275,10 @@
         copy.wait_send()
 
 
+def in_hbm(x):
+    return pltpu.with_memory_space_constraint(x, pltpu.HBM)
+
+
 def shards(
     n_dom,
     n_tm,
@@ -302,8 +306,8 @@
     hidden, weights = pl.pallas_call(
         functools.partial(kernel, n_dom, n_tm),
         out_shape=(
-            jax.ShapeDtypeStruct((rows_dev, width), bf16),
-            jax.ShapeDtypeStruct((width, width), jnp.float32),
+            pltpu.VMEM((rows_dev, width), bf16),
+            pltpu.VMEM((width, width), f32),
         ),
         in_specs=[hbm] * 10,
         out_specs=(vmem, vmem),
@@ -343,19 +347,19 @@
             dma((groups,)),
         ],
         compiler_params=pltpu.CompilerParams(
-            collective_id=0, has_side_effects=True, vmem_limit_bytes=60 * 1024 * 1024
+            collective_id=0, has_side_effects=True, vmem_limit_bytes=48 * 1024 * 1024
         ),
     )(
-        features.reshape(blocks, BLOCK, width),
-        tile_rows,
-        tile_cols,
-        tile_vals.reshape(slots, BLOCK, BLOCK),
+        in_hbm(features.reshape(blocks, BLOCK, width)),
+        in_hbm(tile_rows),
+        in_hbm(tile_cols),
+        in_hbm(tile_vals.reshape(slots, BLOCK, BLOCK)),
         tile_used,
-        pool_weight,
-        w_in,
-        w_state,
-        gate_offset.reshape(1, width),
-        start_weight,
+        in_hbm(pool_weight),
+        in_hbm(w_in),
+        in_hbm(w_state),
+        in_hbm(gate_offset.reshape(1, width)),
+        in_hbm(start_weight),
     )
     return hidden[None], weights[None]
 

time: 35.2 us -> 31.8 us (0.903)
  local copies, waits for them, and re-layouts: 3.93 us -> 1.67 us
  Pallas kernels: 29.8 us -> 28.7 us
    unnamed x2, local copies, waits for them, and re-layouts: 3.93 us -> 1.67 us
    pallas_call x1, Pallas kernels: 29.8 us -> 28.7 us  [shards(): pl.pallas_call(functools.partial(kernel, n_dom, n_tm), out_shape=(pltpu.V...]
where the time goes in v2:
time: 31.8 us; the launch traced here: 31.6 us
  Pallas kernels  28.7 us (90%)
  local copies, waits for them, and re-layouts  1.67 us (5%)
  between operations  1.29 us (4%)
    pallas_call x1, Pallas kernels, shards(): pl.pallas_call(functools.partial(kernel, n_dom, n_tm), out_shape=(pltpu.V...  28.7 us
    unnamed x2, local copies, waits for them, and re-layouts  1.67 us

profile of v2, /device:TPU:0, one launch (start us, length us, event | category | flops | bytes accessed | tf_op | source)
XLA Modules:
  0.0 31.6 jit_solution(9225152284982379030)
XLA Ops:
  1.3 28.7 %shard_map.113 = (bf16[256,512]{1,0:T(8,128)(2,1)S(1)}, f32[512,512]{1,0:T(8,128)S(1)}) custom-call(bf16[2,128,512]{2,1,0:T(8,128)(2,1)} %bitcast.8, s32[1,24]{1,0:T(1,128)} %rows_in.1, s32[1,24]{1,0:T(1,128)} %cols_in.1, bf16[24,128,128]{2,1,0:T(8,128)(2,1)} %bitcast.7, s32[1,1]{1,0:T(1,128)S(6)} %copy.16.used_in, bf16[512,512]{1,0:T(8,128)(2,1)} %pool_ref.1, ...), custom_call_target="tpu_custom_call" | custom-call | tf_op jit(solution)/shard_map/pallas_call | solution.py:306
  30.0 0.7 %copy.14 = bf16[1,256,512]{2,1,0:T(8,128)(2,1)} copy(bf16[1,256,512]{2,1,0:T(8,128)(2,1)S(1)} %bitcast.6) | data formatting | bytes 524288
  30.7 1.0 %copy.15 = f32[1,512,512]{2,1,0:T(8,128)} copy(f32[1,512,512]{2,1,0:T(8,128)S(1)} %bitcast.5) | data formatting | bytes 2097152
